TPU v7x, 32 devices: a whole 2x2x4 slice. The times are simulated.
32 devices in a mesh: tok: 8 (over z, x), hid: 4 (over y, core).
Axes of the slice: x: 2, y: 2, z: 4, core: 2. Of those that a mesh axis runs over, the one named last changes fastest.
Arguments:
- inputs: float32 [1024, 4096], P('tok'), may hold values from -6 to 6
- cotangent: float32 [1024, 4096], P('tok'), may hold values from -6 to 6
- up_blocks: float32 [112, 4, 128, 128], P('hid', None, 'tok'), may hold values from -0.25 to 0.25
- down_blocks: float32 [112, 4, 128, 128], P('hid', None, 'tok'), may hold values from -0.25 to 0.25
- up_index: int32 [112, 4], P('hid'), may hold values from 0 to 31, all different within a row
- down_index: int32 [112, 4], P('hid'), may hold values from 0 to 31, all different within a row
- mom_up: float32 [112, 4, 128, 128], P('hid', None, 'tok'), may hold values from -6 to 6
- mom_down: float32 [112, 4, 128, 128], P('hid', None, 'tok'), may hold values from -6 to 6
Outputs:
- input_grad: float32 [1024, 4096], P('tok', 'hid')
- new_mom_up: float32 [112, 4, 128, 128], P('hid', None, 'tok')
- new_mom_down: float32 [112, 4, 128, 128], P('hid', None, 'tok')
Inputs may be any that keep to these rules, and one draw needn't show every extreme that they name: `up_index`: each row lists 4 different model blocks, and every model block appears in some row. `down_index`: each row lists 4 different model blocks, and every model block appears in some row.
All inputs are finite; a program needn't handle non-finite values.
Results may differ from a plain program's by a relative error of at most 0.0003.
Values sent between devices are 32-bit elements; how exact they have to be, the bound alone decides.
No kernel may reach another device: no remote copies, remote signals or barrier semaphores. Data moves between devices by JAX's collectives and lax.ppermute only.
A program may use at most 128 MiB of HBM per device.

v0:
```python
import functools

import jax
import jax.numpy as jnp
from jax import lax
from jax.experimental import pallas as pl
from jax.experimental.pallas import tpu as pltpu
from jax.sharding import PartitionSpec as P

F32, BF16 = jnp.float32, jnp.bfloat16
NN = (((1,), (0,)), ((), ()))
NT = (((1,), (1,)), ((), ()))


def swap(value, axis, bit):
    size = lax.axis_size(axis)
    return lax.ppermute(value, axis, [(i, i ^ bit) for i in range(size)])


def bits_below(size):
    return [1 << i for i in range(size.bit_length() - 1)]


def inner_size(size):
    inner = 1
    while inner * inner * 8 <= size:
        inner *= 2
    return inner


def split(value):
    high = value.astype(BF16)
    return high, (value - high.astype(F32)).astype(BF16)


def dot(a, b, dims):
    return lax.dot_general(a, b, dims, preferred_element_type=F32)


def kernel(cfg, up_at, down_at, place, *refs):
    starts, sizes, kb, blk, rows, nb, n, q, heads, first, last, awaits = cfg
    fc = sum(sizes)
    refs = list(refs)
    groups = min(n, 2)
    x_own, c_own = refs[:2]
    got, refs = refs[2:2 + 3 * heads], refs[2 + 3 * heads:]
    slabs, refs = refs[:n], refs[n:]
    prev = None
    if not first:
        prev, refs = refs[0], refs[1:]
    refs = refs[awaits:]
    grads = []
    for _ in sizes:
        grads.append(refs[:groups])
        refs = refs[groups:]
    outs, refs = refs[:4 if last else 1], refs[4 if last else 1:]
    w, xb, cb, acc, w_sem, g_sem, x_sem, i_sem = refs
    me, hid = place[0], place[1]
    span = nb // heads

    def weight_copy(r):
        start = pl.multiple_of((me ^ r) * q, q) if n > 1 else 0
        return pltpu.make_async_copy(
            slabs[r].at[:, pl.ds(starts[r], fc)], w.at[:, :, :, pl.ds(start, q), :], w_sem.at[r])

    def grad_copies(act):
        for r in range(n):
            start = pl.multiple_of((me ^ r) * q, q) if n > 1 else 0
            f0 = 0
            for p, size in enumerate(sizes):
                act(pltpu.make_async_copy(
                    w.at[:, pl.ds(f0, size), :, pl.ds(start, q), :],
                    grads[p][r * groups // n].at[r % (n // groups)], g_sem.at[p, r]))
                f0 += size

    def token_copies(f, slot, act):
        for k in range(kb):
            for i, (own, ats, buf) in enumerate(((x_own, up_at, xb), (c_own, down_at, cb))):
                at = ats[f * kb + k]
                col = pl.multiple_of(at * blk, blk)
                act(pltpu.make_async_copy(
                    own.at[:, pl.ds(col, blk)], buf.at[slot, k, pl.ds(0, rows)],
                    x_sem.at[slot, i, k, 0]))
                col = pl.multiple_of(lax.rem(at, span) * blk, blk)
                holder = lax.div(at, span) ^ hid
                for r in range(heads):
                    @pl.when(holder == r)
                    def _():
                        for group in range(1, 4):
                            act(pltpu.make_async_copy(
                                got[(group - 1) * heads + r].at[i, :, pl.ds(col, blk)],
                                buf.at[slot, k, pl.ds(group * rows, rows)],
                                x_sem.at[slot, i, k, group]))

    def start(copy):
        copy.start()

    def wait(copy):
        copy.wait()

    for r in range(n):
        weight_copy(r).start()
    token_copies(0, 0, start)
    if first:
        acc[...] = jnp.zeros_like(acc)
    else:
        fill = pltpu.make_async_copy(prev, acc, i_sem.at[0])
        fill.start()
        fill.wait()
    for r in range(n):
        weight_copy(r).wait()

    def step(f, carry):
        slot = lax.rem(f, 2)

        @pl.when(f + 1 < fc)
        def _():
            token_copies(f + 1, 1 - slot, start)

        token_copies(f, slot, wait)
        xh, xl = split(jnp.concatenate([xb[slot, k] for k in range(kb)], axis=1))
        ch, cl = split(jnp.concatenate([cb[slot, k] for k in range(kb)], axis=1))
        uh, ul = split(w[0, f].reshape(kb * blk, blk))
        dh, dl = split(jnp.concatenate([w[1, f, k] for k in range(kb)], axis=1))

        wide = dot(xh, jnp.concatenate([uh, ul], axis=1), NN)
        pre = wide[:, :blk] + (wide[:, blk:] + dot(xl, uh, NN))
        wide = dot(ch, jnp.concatenate([dh, dl], axis=0), NT)
        grad_act = wide[:, :blk] + (wide[:, blk:] + dot(cl, dh, NT))
        sig = jax.nn.sigmoid(pre)
        act = pre * sig
        grad_pre = grad_act * sig * (1.0 + pre * (1.0 - sig))

        ah, al = split(act.T)
        tall = dot(jnp.concatenate([ah, al], axis=0), ch, NN)
        grad_down = tall[:blk] + (tall[blk:] + dot(ah, cl, NN))
        gh, gl = split(grad_pre.T)
        tall = dot(jnp.concatenate([gh, gl], axis=0), xh, NN)
        grad_up = tall[:blk] + (tall[blk:] + dot(gh, xl, NN))
        ph, plow = split(grad_pre)
        back = dot(jnp.concatenate([ph, plow], axis=1), jnp.concatenate([uh, uh], axis=1), NT)
        back = back + dot(ph, ul, NT)
        for k in range(kb):
            part = slice(k * blk, (k + 1) * blk)
            w[0, f, k] = grad_up[:, part].T
            w[1, f, k] = grad_down[:, part]
            at = up_at[f * kb + k]
            acc[at] = acc[at] + back[:, part]
        return carry

    lax.fori_loop(0, fc, step, 0)
    grad_copies(start)
    if last:
        copies = []
        for r in range(heads):
            for j in range(span):
                for group in range(4):
                    copies.append(pltpu.make_async_copy(
                        acc.at[(hid ^ r) * span + j, pl.ds(group * rows, rows)],
                        outs[2 * (group % 2) + r % 2].at[
                            r // 2, group // 2, :, pl.ds(j * blk, blk)],
                        i_sem.at[len(copies)]))
    else:
        copies = [pltpu.make_async_copy(acc, outs[0], i_sem.at[0])]
    for copy in copies:
        copy.start()
    for copy in copies:
        copy.wait()
    grad_copies(wait)


def block_pass(x, cot, got, slabs, up_at, down_at, me, hid, tok, heads, prev, sizes, last, awaits, loose):
    fc = up_at.shape[0]
    n = len(slabs)
    starts, parts = zip(*slabs)
    kb, q, blk = parts[0].shape[2:]
    rows, width = x.shape
    nb = width // blk
    first = prev is None
    cfg = (starts, sizes, kb, blk, rows, nb, n, q, heads, first, last, len(awaits))
    groups = min(n, 2)
    out = [jax.ShapeDtypeStruct((n // groups, 2, size, kb, q, blk), F32)
           for size in sizes for _ in range(groups)]
    if last:
        out += [jax.ShapeDtypeStruct((heads // 2, 2, rows, width // heads), F32)] * 4
    else:
        out.append(pltpu.HBM((nb, 4 * rows, blk), F32))
    def fixed(*arrays):
        return [pltpu.with_memory_space_constraint(a, pltpu.HBM) for a in arrays]

    parts = [part if loose[r] else fixed(part)[0] for r, part in enumerate(parts)]
    late = {2 * heads - 1, 3 * heads - 2, 3 * heads - 1}
    got = [a if r in late else fixed(a)[0] for r, a in enumerate(got)]
    operands = fixed(x, cot) + got + parts + ([] if first else fixed(prev)) + awaits
    anywhere = pl.BlockSpec(memory_space=pl.ANY)
    products = 4 * rows * fc * kb * blk * blk
    results = pl.pallas_call(
        functools.partial(kernel, cfg),
        out_shape=out,
        grid_spec=pltpu.PrefetchScalarGridSpec(
            num_scalar_prefetch=3,
            grid=(1,),
            in_specs=[anywhere] * len(operands),
            out_specs=[anywhere] * len(out),
            scratch_shapes=[
                pltpu.VMEM((2, fc, kb, blk, blk), F32),
                pltpu.VMEM((2, kb, 4 * rows, blk), F32),
                pltpu.VMEM((2, kb, 4 * rows, blk), F32),
                pltpu.VMEM((nb, 4 * rows, blk), F32),
                pltpu.SemaphoreType.DMA((n,)),
                pltpu.SemaphoreType.DMA((len(sizes), n)),
                pltpu.SemaphoreType.DMA((2, 2, kb, 4)),
                pltpu.SemaphoreType.DMA((4 * nb,)),
            ],
        ),
        compiler_params=pltpu.CompilerParams(vmem_limit_bytes=24 * 2**20),
        cost_estimate=pl.CostEstimate(
            flops=8 * 5 * 3 * products, bytes_accessed=16 * 2**20, transcendentals=0),
    )(up_at.reshape(-1), down_at.reshape(-1), jnp.stack([me, hid]), *operands)
    grads = []
    for p, size in enumerate(sizes):
        pair = results[p * groups:(p + 1) * groups]
        if n == 1:
            whole = pair[0].reshape(2, size, kb, tok, q // tok, blk)
            whole = jnp.take(jnp.moveaxis(whole, 3, 0), me ^ jnp.arange(tok), axis=0)
            whole = whole.reshape((2, tok // 2) + whole.shape[1:])
            pair = whole[0], whole[1]
        grads.append(pair)
    return grads, results[len(sizes) * groups:]


def after(value, *others):
    return lax.optimization_barrier((value, *others))[0]


def shards(inputs, cotangent, up_blocks, down_blocks, up_index, down_index, mom_up, mom_down):
    rows, width = inputs.shape
    blocks, kb, q, blk = up_blocks.shape
    tok, heads = lax.axis_size("tok"), lax.axis_size("hid")
    me, hid = lax.axis_index("tok"), lax.axis_index("hid")
    pair = inner_size(tok)
    most = [b for b in bits_below(tok) if b not in (1, pair)]
    quarter = -(-blocks // 4)
    if quarter * 4 != blocks:
        extra = 4 * quarter - blocks
        up_blocks, down_blocks = (
            jnp.pad(a, ((0, extra), (0, 0), (0, 0), (0, 0))) for a in (up_blocks, down_blocks))
        up_index, down_index = (jnp.pad(a, ((0, extra), (0, 0))) for a in (up_index, down_index))
    cuts = [round(quarter * part / 7) for part in (0, 2, 5, 7)]
    calls = [cuts[:2], cuts[1:]]
    mine = (me // pair) % 2 * 2 + me % 2
    scale = (rows * tok) ** (-0.5)
    span = width // heads

    def weights(which):
        at = which * quarter
        return [lax.dynamic_slice(a, (at, 0, 0, 0), (quarter, kb, q, blk))
                for a in (up_blocks, down_blocks)]

    both = jnp.stack([
        lax.dynamic_slice(a, (0, hid * span), (rows, span)) for a in (inputs, cotangent)])
    x_tokens = swap(both, "tok", 1)
    z_tokens = swap(both, "tok", pair)

    keep = {0: jnp.stack(weights(mine)), pair: jnp.stack(weights(mine ^ 2))}
    give = jnp.stack([jnp.stack(weights(mine ^ 1)), jnp.stack(weights(mine ^ 3))])
    masks = [sum(b for i, b in enumerate(most) if j >> i & 1) for j in range(2 ** len(most))]
    far = [m | p for m in reversed(masks) if m for p in (pair, 0)]

    parts = {0: keep[0]}
    waits = []
    for to in far:
        parts[to] = swap(after(keep[to & pair], *waits), "tok", to)
        waits = [parts[to]]
    given = swap(after(give, x_tokens), "tok", 1)
    parts[1] = given[0]
    second = {0: given[0], pair: given[1]}
    parts[pair] = swap(after(keep[pair], z_tokens), "tok", pair)
    for to in far:
        parts[to | 1] = swap(after(second[to & pair], *waits), "tok", to)
        waits = [parts[to | 1]]
    parts[pair | 1] = swap(after(second[pair], parts[pair]), "tok", pair)

    xz_tokens = swap(after(z_tokens, given), "tok", 1)
    order = [
        (x_tokens, [parts[far[0]]]),
        (z_tokens, [parts[far[-1]]]),
        (xz_tokens, [parts[far[0] | 1], parts[pair]]),
    ]
    got = []
    crossed_y = []
    for fetched, held in order:
        pieces = {0: after(fetched, *held, *crossed_y)}
        for bit in reversed(bits_below(heads)[1:]):
            for r in list(pieces):
                pieces[r | bit] = swap(pieces[r], "hid", bit)
        crossed_y = [pieces[heads - 2]]
        for r in list(pieces):
            pieces[r | 1] = swap(pieces[r], "hid", 1)
        got.append([pieces[r] for r in range(heads)])
    got = got[0] + got[1] + got[2]

    slabs_of = [parts[r] for r in range(tok)]
    total_of, delivered = [], []
    partial, folded = None, []
    for call in calls:
        f0, f1 = call[0], call[-1]
        slabs = [(f0, part) for part in slabs_of]
        if q % 8:
            whole = jnp.stack([part[:, f0:f1] for part in slabs_of])
            whole = jnp.take(whole, me ^ jnp.arange(tok), axis=0)
            slabs = [(0, jnp.moveaxis(whole, 0, 3).reshape(2, f1 - f0, kb, blk, blk))]
        at = (mine * quarter + f0, 0)
        grads, rest = block_pass(
            inputs, cotangent, got, slabs,
            lax.dynamic_slice(up_index, at, (f1 - f0, kb)),
            lax.dynamic_slice(down_index, at, (f1 - f0, kb)),
            me, hid, tok, heads, partial,
            [b - a for a, b in zip(call[:-1], call[1:])], f1 == quarter, [], [True] * tok)
        partial = rest[0]

        for low, high in grads:
            back = swap(after(high, *folded[-1:], *delivered[-1:]), "tok", tok // 2)
            folded.append(back)
            total = low + back
            left = list(reversed(bits_below(tok)))[1:]
            for bit in reversed(most[:-1]):
                p = left.index(bit)
                left.remove(bit)
                total = total.reshape((2 ** p, 2, -1) + total.shape[1:])
                total = (total[:, 0] + swap(total[:, 1], "tok", bit)).reshape(
                    (-1,) + total.shape[3:])
            total_of.append(total)

    handed = {to: [swap(total[r], "tok", to) if to else total[0] for total in total_of]
              for r, to in enumerate((0, 1, pair, pair | 1))}

    shares, firsts = [], folded[:1]
    for x_side in (1, 0):
        even, odd = rest[2 * x_side:2 * x_side + 2]
        first = swap(after(odd, *firsts), "hid", 1)
        total = even + first
        for bit in bits_below(heads)[1:]:
            total = total.reshape((total.shape[0] // 2, 2) + total.shape[1:])
            total = total[:, 0] + swap(total[:, 1], "hid", bit)
        shares.append(total[0])
    share = shares[1] + swap(shares[0], "tok", 1)
    input_grad = share[0] + swap(share[1], "tok", pair)

    quarters = [jnp.concatenate(rows_of, axis=1) for rows_of in handed.values()]
    for bit in (1, 2):
        flip = mine & bit > 0
        quarters = [jnp.where(flip, quarters[j ^ bit], quarters[j]) for j in range(4)]
    ordered = jnp.concatenate(quarters, axis=1)[:, :blocks]
    return (
        input_grad,
        0.9 * mom_up + scale * ordered[0],
        0.9 * mom_down + scale * ordered[1],
    )


def solution(mesh):
    return jax.shard_map(
        shards,
        mesh=mesh,
        in_specs=(
            P("tok", None),
            P("tok", None),
            P("hid", None, "tok", None),
            P("hid", None, "tok", None),
            P("hid", None),
            P("hid", None),
            P("hid", None, "tok", None),
            P("hid", None, "tok", None),
        ),
        out_specs=(P("tok", "hid"), P("hid", None, "tok", None), P("hid", None, "tok", None)),
        check_vma=False,
    )
```

profile of v0, /device:TPU:0, one launch (start us, length us, event | category | flops | bytes accessed | tf_op | source)
XLA Modules:
  0.0 239.1 jit_solution(18131786118587728074)
XLA Ops:
  2.2 3.0 %collective-permute-start = (f32[2,128,1024]{2,1,0:T(8,128)S(1)}, f32[2,128,1024]{2,1,0:T(8,128)}, u32[]{:S(2)}, u32[]{:S(2)}) collective-permute-start(f32[2,128,1024]{2,1,0:T(8,128)S(1)} %pad_maximum_fusion.1), channel_id=1, source_target_pairs={{0,4},{4,0},{8,12},{12,8},{16,20},{20,16},{24,28},{28,24},{1,5},{5... | collective-permute-start | bytes 3145736 | tf_op jit(solution)/shard_map/ppermute | solution.py:17
  5.4 3.7 %collective-permute-start.1 = (f32[2,7,4,16,128]{4,3,2,1,0:T(8,128)S(1)}, f32[2,7,4,16,128]{4,3,2,1,0:T(8,128)S(1)}, u32[]{:S(2)}, u32[]{:S(2)}) collective-permute-start(f32[2,7,4,16,128]{4,3,2,1,0:T(8,128)S(1)} %pad_maximum_fusion.3), channel_id=1, source_target_pairs={{0,24},{4,28},{8,16},{12,20},{16,8},{20,12},{24,0},{28,4},{1,25},{... | collective-permute-start | bytes 1376264 | tf_op jit(solution)/shard_map/ppermute | solution.py:17
  9.1 11.6 %collective-permute-done.1.refs_20_ = f32[2,7,4,16,128]{4,3,2,1,0:T(8,128)S(1)} collective-permute-done((f32[2,7,4,16,128]{4,3,2,1,0:T(8,128)S(1)}, f32[2,7,4,16,128]{4,3,2,1,0:T(8,128)S(1)}, u32[]{:S(2)}, u32[]{:S(2)}) %collective-permute-start.1) | collective-permute-done | bytes 458784 | tf_op jit(solution)/shard_map/ppermute | solution.py:17
  21.5 7.0 %collective-permute-done.refs_2_ = f32[2,128,1024]{2,1,0:T(8,128)} collective-permute-done((f32[2,128,1024]{2,1,0:T(8,128)S(1)}, f32[2,128,1024]{2,1,0:T(8,128)}, u32[]{:S(2)}, u32[]{:S(2)}) %collective-permute-start) | collective-permute-done | bytes 1048608 | tf_op jit(solution)/shard_map/ppermute | solution.py:17
  28.4 1.8 collective-permute-start.3
  30.3 1.6 collective-permute-start.10
  31.9 2.7 %collective-permute-start.6 = (f32[2,7,4,16,128]{4,3,2,1,0:T(8,128)S(1)}, f32[2,7,4,16,128]{4,3,2,1,0:T(8,128)S(1)}, u32[]{:S(2)}, u32[]{:S(2)}) collective-permute-start(f32[2,7,4,16,128]{4,3,2,1,0:T(8,128)S(1)} %pad_maximum_fusion.4.refs_14_), channel_id=1, source_target_pairs={{0,16},{4,20},{8,24},{12,28},{16,0},{20,4},{24,8},{28,12},{1,17},{... | collective-permute-start | bytes 1376264 | tf_op jit(solution)/shard_map/ppermute | solution.py:17
  34.6 15.4 %collective-permute-done.5.refs_6_ = f32[2,128,1024]{2,1,0:T(8,128)} collective-permute-done((f32[2,128,1024]{2,1,0:T(8,128)S(1)}, f32[2,128,1024]{2,1,0:T(8,128)}, u32[]{:S(2)}, u32[]{:S(2)}) %collective-permute-start.5) | collective-permute-done | bytes 1048608 | tf_op jit(solution)/shard_map/ppermute | solution.py:17
  51.3 1.5 collective-permute-start.11
  56.2 2.5 %collective-permute-start.12 = (f32[2,7,4,16,128]{4,3,2,1,0:T(8,128)S(1)}, f32[2,7,4,16,128]{4,3,2,1,0:T(8,128)S(1)}, u32[]{:S(2)}, u32[]{:S(2)}) collective-permute-start(f32[2,7,4,16,128]{4,3,2,1,0:T(8,128)S(1)} %get-tuple-element.36), channel_id=1, source_target_pairs={{0,24},{4,28},{8,16},{12,20},{16,8},{20,12},{24,0},{28,4},{1,25},{... | collective-permute-start | bytes 1376264 | tf_op jit(solution)/shard_map/ppermute | solution.py:17
  58.8 8.7 %collective-permute-done.13.refs_16_ = f32[2,7,4,16,128]{4,3,2,1,0:T(8,128)S(1)} collective-permute-done((f32[2,7,4,16,128]{4,3,2,1,0:T(8,128)S(1)}, f32[2,7,4,16,128]{4,3,2,1,0:T(8,128)S(1)}, u32[]{:S(2)}, u32[]{:S(2)}) %collective-permute-start.13) | collective-permute-done | bytes 458784 | tf_op jit(solution)/shard_map/ppermute | solution.py:17
  68.3 8.5 %collective-permute-done.12.refs_21_ = f32[2,7,4,16,128]{4,3,2,1,0:T(8,128)S(1)} collective-permute-done((f32[2,7,4,16,128]{4,3,2,1,0:T(8,128)S(1)}, f32[2,7,4,16,128]{4,3,2,1,0:T(8,128)S(1)}, u32[]{:S(2)}, u32[]{:S(2)}) %collective-permute-start.12) | collective-permute-done | bytes 458784 | tf_op jit(solution)/shard_map/ppermute | solution.py:17
  79.6 2.8 %collective-permute-start.18 = (f32[2,7,4,16,128]{4,3,2,1,0:T(8,128)S(1)}, f32[2,7,4,16,128]{4,3,2,1,0:T(8,128)S(1)}, u32[]{:S(2)}, u32[]{:S(2)}) collective-permute-start(f32[2,7,4,16,128]{4,3,2,1,0:T(8,128)S(1)} %get-tuple-element.37.refs_15_), channel_id=1, source_target_pairs={{0,16},{4,20},{8,24},{12,28},{16,0},{20,4},{24,8},{28,12},{1,17},{... | collective-permute-start | bytes 1376264 | tf_op jit(solution)/shard_map/ppermute | solution.py:17
  82.9 15.6 %collective-permute-done.17.refs_17_ = f32[2,7,4,16,128]{4,3,2,1,0:T(8,128)S(1)} collective-permute-done((f32[2,7,4,16,128]{4,3,2,1,0:T(8,128)S(1)}, f32[2,7,4,16,128]{4,3,2,1,0:T(8,128)S(1)}, u32[]{:S(2)}, u32[]{:S(2)}) %collective-permute-start.17) | collective-permute-done | bytes 458784 | tf_op jit(solution)/shard_map/ppermute | solution.py:17
  102.2 2.1 collective-permute-done.9.refs_9_
  111.2 10.7 %shard_map.103 = (f32[4,2,2,4,16,128]{5,4,3,2,1,0:T(8,128)S(1)}, f32[4,2,2,4,16,128]{5,4,3,2,1,0:T(8,128)S(1)}, f32[32,512,128]{2,1,0:T(8,128)}) custom-call(s32[8]{0:T(128)S(1)} %reshape.30.up_at, s32[8]{0:T(128)S(1)} %reshape.31.down_at, s32[2]{0:T(128)S(1)} %pad_add_fusion.place, f32[128,4096]{1,0:T(8,128)} %refs_0_.3, f32[128,4096]{1,0:T(8,128)} %refs_1_.3, ...), custom_call_target="tpu_custom_call" | custom-call | flops 8053063680 | bytes 16777216 | tf_op jit(solution)/shard_map/pallas_call | solution.py:197
  127.5 18.7 %shard_map.104 = (f32[4,2,3,4,16,128]{5,4,3,2,1,0:T(8,128)S(1)}, f32[4,2,3,4,16,128]{5,4,3,2,1,0:T(8,128)S(1)}, f32[4,2,2,4,16,128]{5,4,3,2,1,0:T(8,128)S(1)}, f...) custom-call(s32[20]{0:T(128)S(1)} %reshape.28.up_at, ...), custom_call_target="tpu_custom_call" | custom-call | flops 20132659200 | bytes 16777216 | tf_op jit(solution)/shard_map/pallas_call | solution.py:197
  149.8 2.6 %collective-permute-start.27 = (f32[4,2,3,4,16,128]{5,4,3,2,1,0:T(8,128)}, f32[4,2,3,4,16,128]{5,4,3,2,1,0:T(8,128)S(1)}, u32[]{:S(2)}, u32[]{:S(2)}) collective-permute-start(f32[4,2,3,4,16,128]{5,4,3,2,1,0:T(8,128)} %copy-done.11), channel_id=1, source_target_pairs={{0,16},{4,20},{8,24},{12,28},{16,0},{20,4},{24,8},{28,12},{1,17},{... | collective-permute-start | bytes 2359304 | tf_op jit(solution)/shard_map/ppermute | solution.py:17
  153.8 1.5 collective-permute-start.34
  155.3 2.0 collective-permute-start.26
  157.3 2.0 add_bitcast_fusion
  159.9 13.6 %collective-permute-done.31 = f32[2,2,4,16,128]{4,3,2,1,0:T(8,128)S(1)} collective-permute-done((f32[2,2,4,16,128]{4,3,2,1,0:T(8,128)S(1)}, f32[2,2,4,16,128]{4,3,2,1,0:T(8,128)S(1)}, u32[]{:S(2)}, u32[]{:S(2)}) %collective-permute-start.31) | collective-permute-done | bytes 131104 | tf_op jit(solution)/shard_map/ppermute | solution.py:17
  173.4 13.8 %collective-permute-done.27 = f32[4,2,3,4,16,128]{5,4,3,2,1,0:T(8,128)S(1)} collective-permute-done((f32[4,2,3,4,16,128]{5,4,3,2,1,0:T(8,128)}, f32[4,2,3,4,16,128]{5,4,3,2,1,0:T(8,128)S(1)}, u32[]{:S(2)}, u32[]{:S(2)}) %collective-permute-start.27) | collective-permute-done | bytes 786464 | tf_op jit(solution)/shard_map/ppermute | solution.py:17
  187.5 1.5 collective-permute-start.35
  188.9 2.0 add_bitcast_fusion.1
  192.5 2.4 collective-permute-start.32
  196.0 17.2 %collective-permute-done.29 = f32[4,2,2,4,16,128]{5,4,3,2,1,0:T(8,128)S(1)} collective-permute-done((f32[4,2,2,4,16,128]{5,4,3,2,1,0:T(8,128)S(1)}, f32[4,2,2,4,16,128]{5,4,3,2,1,0:T(8,128)S(1)}, u32[]{:S(2)}, u32[]{:S(2)}) %collective-permute-start.29) | collective-permute-done | bytes 524320 | tf_op jit(solution)/shard_map/ppermute | solution.py:17
  214.4 2.6 %collective-permute-start.30 = (f32[2,2,4,16,128]{4,3,2,1,0:T(8,128)S(1)}, f32[2,2,4,16,128]{4,3,2,1,0:T(8,128)S(1)}, u32[]{:S(2)}, u32[]{:S(2)}) collective-permute-start(f32[2,2,4,16,128]{4,3,2,1,0:T(8,128)S(1)} %get-tuple-element.80), channel_id=1, source_target_pairs={{0,12},{4,8},{8,4},{12,0},{16,28},{20,24},{24,20},{28,16},{1,13},{... | collective-permute-start | bytes 393224 | tf_op jit(solution)/shard_map/ppermute | solution.py:17
  217.0 8.7 %collective-permute-done.36 = f32[2,2,4,16,128]{4,3,2,1,0:T(8,128)S(1)} collective-permute-done((f32[2,2,4,16,128]{4,3,2,1,0:T(8,128)S(1)}, f32[2,2,4,16,128]{4,3,2,1,0:T(8,128)S(1)}, u32[]{:S(2)}, u32[]{:S(2)}) %collective-permute-start.36) | collective-permute-done | bytes 131104 | tf_op jit(solution)/shard_map/ppermute | solution.py:17
  226.2 1.8 collective-permute-start.25
  229.8 1.6 fusion.6
  231.4 6.9 %collective-permute-done.25 = f32[128,1024]{1,0:T(8,128)S(1)} collective-permute-done((f32[128,1024]{1,0:T(8,128)S(1)}, f32[128,1024]{1,0:T(8,128)S(1)}, u32[]{:S(2)}, u32[]{:S(2)}) %collective-permute-start.25) | collective-permute-done | bytes 524320 | tf_op jit(solution)/shard_map/ppermute | solution.py:17
  (168 shorter events, 40.1 us)
Async XLA Ops:
  2.2 26.3 %collective-permute-start = (f32[2,128,1024]{2,1,0:T(8,128)S(1)}, f32[2,128,1024]{2,1,0:T(8,128)}, u32[]{:S(2)}, u32[]{:S(2)}) collective-permute-start(f32[2,128,1024]{2,1,0:T(8,128)S(1)} %pad_maximum_fusion.1), channel_id=1, source_target_pairs={{0,4},{4,0},{8,12},{12,8},{16,20},{20,16},{24,28},{28,24},{1,5},{5... | collective-permute-start | bytes 3145736 | tf_op jit(solution)/shard_map/ppermute | solution.py:17
  5.4 15.3 %collective-permute-start.1 = (f32[2,7,4,16,128]{4,3,2,1,0:T(8,128)S(1)}, f32[2,7,4,16,128]{4,3,2,1,0:T(8,128)S(1)}, u32[]{:S(2)}, u32[]{:S(2)}) collective-permute-start(f32[2,7,4,16,128]{4,3,2,1,0:T(8,128)S(1)} %pad_maximum_fusion.3), channel_id=1, source_target_pairs={{0,24},{4,28},{8,16},{12,20},{16,8},{20,12},{24,0},{28,4},{1,25},{... | collective-permute-start | bytes 1376264 | tf_op jit(solution)/shard_map/ppermute | solution.py:17
  9.0 40.9 %collective-permute-start.5 = (f32[2,128,1024]{2,1,0:T(8,128)S(1)}, f32[2,128,1024]{2,1,0:T(8,128)}, u32[]{:S(2)}, u32[]{:S(2)}) collective-permute-start(f32[2,128,1024]{2,1,0:T(8,128)S(1)} %pad_maximum_fusion.1), channel_id=1, source_target_pairs={{0,8},{4,12},{8,0},{12,4},{16,24},{20,28},{24,16},{28,20},{1,9},{5... | collective-permute-start | bytes 3145736 | tf_op jit(solution)/shard_map/ppermute | solution.py:17
  28.4 25.9 %collective-permute-start.3 = (f32[2,128,1024]{2,1,0:T(8,128)}, f32[2,128,1024]{2,1,0:T(8,128)}, u32[]{:S(2)}, u32[]{:S(2)}) collective-permute-start(f32[2,128,1024]{2,1,0:T(8,128)} %collective-permute-done.refs_2_), channel_id=1, source_target_pairs={{0,2},{1,3},{2,0},{3,1},{4,6},{5,7},{6,4},{7,5},{8,10},{9,11},{10,... | collective-permute-start | bytes 3145736 | tf_op jit(solution)/shard_map/ppermute | solution.py:17
  30.3 21.0 %collective-permute-start.10 = (f32[2,2,7,4,16,128]{5,4,3,2,1,0:T(8,128)S(1)}, f32[2,2,7,4,16,128]{5,4,3,2,1,0:T(8,128)S(1)}, u32[]{:S(2)}, u32[]{:S(2)}) collective-permute-start(f32[2,2,7,4,16,128]{5,4,3,2,1,0:T(8,128)S(1)} %pad_maximum_fusion.2), channel_id=1, source_target_pairs={{0,4},{4,0},{8,12},{12,8},{16,20},{20,16},{24,28},{28,24},{1,5},{5... | collective-permute-start | bytes 2752520 | tf_op jit(solution)/shard_map/ppermute | solution.py:17
  31.9 21.7 %collective-permute-start.6 = (f32[2,7,4,16,128]{4,3,2,1,0:T(8,128)S(1)}, f32[2,7,4,16,128]{4,3,2,1,0:T(8,128)S(1)}, u32[]{:S(2)}, u32[]{:S(2)}) collective-permute-start(f32[2,7,4,16,128]{4,3,2,1,0:T(8,128)S(1)} %pad_maximum_fusion.4.refs_14_), channel_id=1, source_target_pairs={{0,16},{4,20},{8,24},{12,28},{16,0},{20,4},{24,8},{28,12},{1,17},{... | collective-permute-start | bytes 1376264 | tf_op jit(solution)/shard_map/ppermute | solution.py:17
  51.3 26.3 %collective-permute-start.11 = (f32[2,128,1024]{2,1,0:T(8,128)}, f32[2,128,1024]{2,1,0:T(8,128)}, u32[]{:S(2)}, u32[]{:S(2)}) collective-permute-start(f32[2,128,1024]{2,1,0:T(8,128)} %collective-permute-done.5.refs_6_), channel_id=1, source_target_pairs={{0,4},{4,0},{8,12},{12,8},{16,20},{20,16},{24,28},{28,24},{1,5},{5... | collective-permute-start | bytes 3145736 | tf_op jit(solution)/shard_map/ppermute | solution.py:17
  54.4 23.2 %collective-permute-start.8 = (f32[2,128,1024]{2,1,0:T(8,128)}, f32[2,128,1024]{2,1,0:T(8,128)}, u32[]{:S(2)}, u32[]{:S(2)}) collective-permute-start(f32[2,128,1024]{2,1,0:T(8,128)} %collective-permute-done.5.refs_6_), channel_id=1, source_target_pairs={{0,2},{1,3},{2,0},{3,1},{4,6},{5,7},{6,4},{7,5},{8,10},{9,11},{10,... | collective-permute-start | bytes 3145736 | tf_op jit(solution)/shard_map/ppermute | solution.py:17
  54.9 12.7 %collective-permute-start.13 = (f32[2,7,4,16,128]{4,3,2,1,0:T(8,128)S(1)}, f32[2,7,4,16,128]{4,3,2,1,0:T(8,128)S(1)}, u32[]{:S(2)}, u32[]{:S(2)}) collective-permute-start(f32[2,7,4,16,128]{4,3,2,1,0:T(8,128)S(1)} %pad_maximum_fusion.3), channel_id=1, source_target_pairs={{0,8},{4,12},{8,0},{12,4},{16,24},{20,28},{24,16},{28,20},{1,9},{5... | collective-permute-start | bytes 1376264 | tf_op jit(solution)/shard_map/ppermute | solution.py:17
  56.2 20.6 %collective-permute-start.12 = (f32[2,7,4,16,128]{4,3,2,1,0:T(8,128)S(1)}, f32[2,7,4,16,128]{4,3,2,1,0:T(8,128)S(1)}, u32[]{:S(2)}, u32[]{:S(2)}) collective-permute-start(f32[2,7,4,16,128]{4,3,2,1,0:T(8,128)S(1)} %get-tuple-element.36), channel_id=1, source_target_pairs={{0,24},{4,28},{8,16},{12,20},{16,8},{20,12},{24,0},{28,4},{1,25},{... | collective-permute-start | bytes 1376264 | tf_op jit(solution)/shard_map/ppermute | solution.py:17
  58.8 23.6 %collective-permute-start.2 = (f32[2,128,1024]{2,1,0:T(8,128)}, f32[2,128,1024]{2,1,0:T(8,128)S(1)}, u32[]{:S(2)}, u32[]{:S(2)}) collective-permute-start(f32[2,128,1024]{2,1,0:T(8,128)} %collective-permute-done.refs_2_), channel_id=1, source_target_pairs={{0,1},{1,0},{2,3},{3,2},{4,5},{5,4},{6,7},{7,6},{8,9},{9,8},{10,11... | collective-permute-start | bytes 3145736 | tf_op jit(solution)/shard_map/ppermute | solution.py:17
  77.6 23.2 %collective-permute-start.15 = (f32[2,128,1024]{2,1,0:T(8,128)}, f32[2,128,1024]{2,1,0:T(8,128)S(1)}, u32[]{:S(2)}, u32[]{:S(2)}) collective-permute-start(f32[2,128,1024]{2,1,0:T(8,128)} %collective-permute-done.11.refs_10_), channel_id=1, source_target_pairs={{0,2},{1,3},{2,0},{3,1},{4,6},{5,7},{6,4},{7,5},{8,10},{9,11},{10,... | collective-permute-start | bytes 3145736 | tf_op jit(solution)/shard_map/ppermute | solution.py:17
  78.8 19.6 %collective-permute-start.17 = (f32[2,7,4,16,128]{4,3,2,1,0:T(8,128)S(1)}, f32[2,7,4,16,128]{4,3,2,1,0:T(8,128)S(1)}, u32[]{:S(2)}, u32[]{:S(2)}) collective-permute-start(f32[2,7,4,16,128]{4,3,2,1,0:T(8,128)S(1)} %get-tuple-element.36), channel_id=1, source_target_pairs={{0,8},{4,12},{8,0},{12,4},{16,24},{20,28},{24,16},{28,20},{1,9},{5... | collective-permute-start | bytes 1376264 | tf_op jit(solution)/shard_map/ppermute | solution.py:17
  79.6 20.4 %collective-permute-start.18 = (f32[2,7,4,16,128]{4,3,2,1,0:T(8,128)S(1)}, f32[2,7,4,16,128]{4,3,2,1,0:T(8,128)S(1)}, u32[]{:S(2)}, u32[]{:S(2)}) collective-permute-start(f32[2,7,4,16,128]{4,3,2,1,0:T(8,128)S(1)} %get-tuple-element.37.refs_15_), channel_id=1, source_target_pairs={{0,16},{4,20},{8,24},{12,28},{16,0},{20,4},{24,8},{28,12},{1,17},{... | collective-permute-start | bytes 1376264 | tf_op jit(solution)/shard_map/ppermute | solution.py:17
  82.4 19.8 %collective-permute-start.7 = (f32[2,128,1024]{2,1,0:T(8,128)}, f32[2,128,1024]{2,1,0:T(8,128)}, u32[]{:S(2)}, u32[]{:S(2)}) collective-permute-start(f32[2,128,1024]{2,1,0:T(8,128)} %collective-permute-done.5.refs_6_), channel_id=1, source_target_pairs={{0,1},{1,0},{2,3},{3,2},{4,5},{5,4},{6,7},{7,6},{8,9},{9,8},{10,11... | collective-permute-start | bytes 3145736 | tf_op jit(solution)/shard_map/ppermute | solution.py:17
  82.4 19.8 %collective-permute-start.4 = (f32[2,128,1024]{2,1,0:T(8,128)}, f32[2,128,1024]{2,1,0:T(8,128)}, u32[]{:S(2)}, u32[]{:S(2)}) collective-permute-start(f32[2,128,1024]{2,1,0:T(8,128)} %collective-permute-done.3.refs_4_), channel_id=1, source_target_pairs={{0,1},{1,0},{2,3},{3,2},{4,5},{5,4},{6,7},{7,6},{8,9},{9,8},{10,11... | collective-permute-start | bytes 3145736 | tf_op jit(solution)/shard_map/ppermute | solution.py:17
  122.7 26.6 %collective-permute-start.19 = (f32[4,2,2,4,16,128]{5,4,3,2,1,0:T(8,128)S(1)}, f32[4,2,2,4,16,128]{5,4,3,2,1,0:T(8,128)}, u32[]{:S(2)}, u32[]{:S(2)}) collective-permute-start(f32[4,2,2,4,16,128]{5,4,3,2,1,0:T(8,128)S(1)} %get-tuple-element.41), channel_id=1, source_target_pairs={{0,16},{4,20},{8,24},{12,28},{16,0},{20,4},{24,8},{28,12},{1,17},{... | collective-permute-start | bytes 1572872 | tf_op jit(solution)/shard_map/ppermute | solution.py:17
  149.3 39.6 %collective-permute-start.20 = (f32[2,2,128,1024]{3,2,1,0:T(8,128)}, f32[2,2,128,1024]{3,2,1,0:T(8,128)}, u32[]{:S(2)}, u32[]{:S(2)}) collective-permute-start(f32[2,2,128,1024]{3,2,1,0:T(8,128)} %get-tuple-element.42), channel_id=1, source_target_pairs={{0,1},{1,0},{2,3},{3,2},{4,5},{5,4},{6,7},{7,6},{8,9},{9,8},{10,11... | collective-permute-start | bytes 6291464 | tf_op jit(solution)/shard_map/ppermute | solution.py:17
  149.8 37.4 %collective-permute-start.27 = (f32[4,2,3,4,16,128]{5,4,3,2,1,0:T(8,128)}, f32[4,2,3,4,16,128]{5,4,3,2,1,0:T(8,128)S(1)}, u32[]{:S(2)}, u32[]{:S(2)}) collective-permute-start(f32[4,2,3,4,16,128]{5,4,3,2,1,0:T(8,128)} %copy-done.11), channel_id=1, source_target_pairs={{0,16},{4,20},{8,24},{12,28},{16,0},{20,4},{24,8},{28,12},{1,17},{... | collective-permute-start | bytes 2359304 | tf_op jit(solution)/shard_map/ppermute | solution.py:17
  155.2 18.2 %collective-permute-start.31 = (f32[2,2,4,16,128]{4,3,2,1,0:T(8,128)S(1)}, f32[2,2,4,16,128]{4,3,2,1,0:T(8,128)S(1)}, u32[]{:S(2)}, u32[]{:S(2)}) collective-permute-start(f32[2,2,4,16,128]{4,3,2,1,0:T(8,128)S(1)} %get-tuple-element.75), channel_id=1, source_target_pairs={{0,8},{4,12},{8,0},{12,4},{16,24},{20,28},{24,16},{28,20},{1,9},{5... | collective-permute-start | bytes 393224 | tf_op jit(solution)/shard_map/ppermute | solution.py:17
  155.3 37.2 %collective-permute-start.26 = (f32[2,2,4,16,128]{4,3,2,1,0:T(8,128)S(1)}, f32[2,2,4,16,128]{4,3,2,1,0:T(8,128)S(1)}, u32[]{:S(2)}, u32[]{:S(2)}) collective-permute-start(f32[2,2,4,16,128]{4,3,2,1,0:T(8,128)S(1)} %get-tuple-element.76), channel_id=1, source_target_pairs={{0,12},{4,8},{8,4},{12,0},{16,28},{20,24},{24,20},{28,16},{1,13},{... | collective-permute-start | bytes 393224 | tf_op jit(solution)/shard_map/ppermute | solution.py:17
  159.4 32.2 %collective-permute-start.23 = (f32[1,2,128,1024]{3,2,1,0:T(8,128)S(1)}, f32[1,2,128,1024]{3,2,1,0:T(8,128)S(1)}, u32[]{:S(2)}, u32[]{:S(2)}) collective-permute-start(f32[1,2,128,1024]{3,2,1,0:T(8,128)S(1)} %slice_bitcast_fusion), channel_id=1, source_target_pairs={{0,2},{1,3},{2,0},{3,1},{4,6},{5,7},{6,4},{7,5},{8,10},{9,11},{10,... | collective-permute-start | bytes 3145736 | tf_op jit(solution)/shard_map/ppermute | solution.py:17
  187.5 7.5 %collective-permute-start.35 = (f32[2,3,4,16,128]{4,3,2,1,0:T(8,128)S(1)}, f32[2,3,4,16,128]{4,3,2,1,0:T(8,128)S(1)}, u32[]{:S(2)}, u32[]{:S(2)}) collective-permute-start(f32[2,3,4,16,128]{4,3,2,1,0:T(8,128)S(1)} %get-tuple-element.70), channel_id=1, source_target_pairs={{0,4},{4,0},{8,12},{12,8},{16,20},{20,16},{24,28},{28,24},{1,5},{5... | collective-permute-start | bytes 589832 | tf_op jit(solution)/shard_map/ppermute | solution.py:17
  188.9 24.2 %collective-permute-start.29 = (f32[4,2,2,4,16,128]{5,4,3,2,1,0:T(8,128)S(1)}, f32[4,2,2,4,16,128]{5,4,3,2,1,0:T(8,128)S(1)}, u32[]{:S(2)}, u32[]{:S(2)}) collective-permute-start(f32[4,2,2,4,16,128]{5,4,3,2,1,0:T(8,128)S(1)} %copy-done.13), channel_id=1, source_target_pairs={{0,16},{4,20},{8,24},{12,28},{16,0},{20,4},{24,8},{28,12},{1,17},{... | collective-permute-start | bytes 1572872 | tf_op jit(solution)/shard_map/ppermute | solution.py:17
  191.0 34.8 %collective-permute-start.21 = (f32[1,2,128,1024]{3,2,1,0:T(8,128)S(1)}, f32[1,2,128,1024]{3,2,1,0:T(8,128)S(1)}, u32[]{:S(2)}, u32[]{:S(2)}) collective-permute-start(f32[1,2,128,1024]{3,2,1,0:T(8,128)S(1)} %slice_bitcast_fusion.2), channel_id=1, source_target_pairs={{0,2},{1,3},{2,0},{3,1},{4,6},{5,7},{6,4},{7,5},{8,10},{9,11},{10,... | collective-permute-start | bytes 3145736 | tf_op jit(solution)/shard_map/ppermute | solution.py:17
  191.8 34.1 %collective-permute-start.24 = (f32[2,128,1024]{2,1,0:T(8,128)S(1)}, f32[2,128,1024]{2,1,0:T(8,128)S(1)}, u32[]{:S(2)}, u32[]{:S(2)}) collective-permute-start(f32[2,128,1024]{2,1,0:T(8,128)S(1)} %fusion.1), channel_id=1, source_target_pairs={{0,4},{4,0},{8,12},{12,8},{16,20},{20,16},{24,28},{28,24},{1,5},{5... | collective-permute-start | bytes 3145736 | tf_op jit(solution)/shard_map/ppermute | solution.py:17
  192.5 21.6 %collective-permute-start.32 = (f32[2,3,4,16,128]{4,3,2,1,0:T(8,128)S(1)}, f32[2,3,4,16,128]{4,3,2,1,0:T(8,128)S(1)}, u32[]{:S(2)}, u32[]{:S(2)}) collective-permute-start(f32[2,3,4,16,128]{4,3,2,1,0:T(8,128)S(1)} %get-tuple-element.71), channel_id=1, source_target_pairs={{0,8},{4,12},{8,0},{12,4},{16,24},{20,28},{24,16},{28,20},{1,9},{5... | collective-permute-start | bytes 589832 | tf_op jit(solution)/shard_map/ppermute | solution.py:17
  194.9 19.5 %collective-permute-start.28 = (f32[2,3,4,16,128]{4,3,2,1,0:T(8,128)S(1)}, f32[2,3,4,16,128]{4,3,2,1,0:T(8,128)S(1)}, u32[]{:S(2)}, u32[]{:S(2)}) collective-permute-start(f32[2,3,4,16,128]{4,3,2,1,0:T(8,128)S(1)} %get-tuple-element.72), channel_id=1, source_target_pairs={{0,12},{4,8},{8,4},{12,0},{16,28},{20,24},{24,20},{28,16},{1,13},{... | collective-permute-start | bytes 589832 | tf_op jit(solution)/shard_map/ppermute | solution.py:17
  213.3 12.5 %collective-permute-start.36 = (f32[2,2,4,16,128]{4,3,2,1,0:T(8,128)S(1)}, f32[2,2,4,16,128]{4,3,2,1,0:T(8,128)S(1)}, u32[]{:S(2)}, u32[]{:S(2)}) collective-permute-start(f32[2,2,4,16,128]{4,3,2,1,0:T(8,128)S(1)} %get-tuple-element.78), channel_id=1, source_target_pairs={{0,4},{4,0},{8,12},{12,8},{16,20},{20,16},{24,28},{28,24},{1,5},{5... | collective-permute-start | bytes 393224 | tf_op jit(solution)/shard_map/ppermute | solution.py:17
  214.2 11.6 %collective-permute-start.33 = (f32[2,2,4,16,128]{4,3,2,1,0:T(8,128)S(1)}, f32[2,2,4,16,128]{4,3,2,1,0:T(8,128)S(1)}, u32[]{:S(2)}, u32[]{:S(2)}) collective-permute-start(f32[2,2,4,16,128]{4,3,2,1,0:T(8,128)S(1)} %get-tuple-element.79), channel_id=1, source_target_pairs={{0,8},{4,12},{8,0},{12,4},{16,24},{20,28},{24,16},{28,20},{1,9},{5... | collective-permute-start | bytes 393224 | tf_op jit(solution)/shard_map/ppermute | solution.py:17
  214.4 11.4 %collective-permute-start.30 = (f32[2,2,4,16,128]{4,3,2,1,0:T(8,128)S(1)}, f32[2,2,4,16,128]{4,3,2,1,0:T(8,128)S(1)}, u32[]{:S(2)}, u32[]{:S(2)}) collective-permute-start(f32[2,2,4,16,128]{4,3,2,1,0:T(8,128)S(1)} %get-tuple-element.80), channel_id=1, source_target_pairs={{0,12},{4,8},{8,4},{12,0},{16,28},{20,24},{24,20},{28,16},{1,13},{... | collective-permute-start | bytes 393224 | tf_op jit(solution)/shard_map/ppermute | solution.py:17
  226.2 12.0 %collective-permute-start.25 = (f32[128,1024]{1,0:T(8,128)S(1)}, f32[128,1024]{1,0:T(8,128)S(1)}, u32[]{:S(2)}, u32[]{:S(2)}) collective-permute-start(f32[128,1024]{1,0:T(8,128)S(1)} %slice_bitcast_fusion.4), channel_id=1, source_target_pairs={{0,8},{4,12},{8,0},{12,4},{16,24},{20,28},{24,16},{28,20},{1,9},{5... | collective-permute-start | bytes 1572872 | tf_op jit(solution)/shard_map/ppermute | solution.py:17
  (44 other events, 556.6 us)
where the time goes:
time: 240 us; the launch traced here: 239 us
  waiting for transfers between devices  133 us (55%)
  starting transfers between devices  43.2 us (18%)
  Pallas kernels  29.4 us (12%)
  local copies, waits for them, and re-layouts  23.3 us (10%)
  other arithmetic  9.19 us (4%)
    ppermute x37, waiting for transfers between devices, swap(): return lax.ppermute(value, axis, [(i, i ^ bit) for i in range(size)])  133 us
    ppermute x37, starting transfers between devices, swap(): return lax.ppermute(value, axis, [(i, i ^ bit) for i in range(size)])  43.2 us
    pallas_call x2, Pallas kernels, block_pass(): pl.pallas_call(functools.partial(kernel, cfg), out_shape=out, grid_spec=p...  29.4 us
    unnamed x84, local copies, waits for them, and re-layouts  20.4 us
  transfers between devices with their start and end apart: 37, of which 17 were waited for; matrix products, arithmetic and copies ran while one was open for 4% of the time, Pallas kernels for 8%

commit v1 on v0

--- a/solution.py
+++ b/solution.py
@@ -316,7 +316,7 @@
             lax.dynamic_slice(up_index, at, (f1 - f0, kb)),
             lax.dynamic_slice(down_index, at, (f1 - f0, kb)),
             me, hid, tok, heads, partial,
-            [b - a for a, b in zip(call[:-1], call[1:])], f1 == quarter, [], [True] * tok)
+            [b - a for a, b in zip(call[:-1], call[1:])], f1 == quarter, [], [False] * tok)
         partial = rest[0]
 
         for low, high in grads:
@@ -332,9 +332,12 @@
                     (-1,) + total.shape[3:])
             total_of.append(total)
 
-    handed = {to: [swap(total[r], "tok", to) if to else total[0] for total in total_of]
-              for r, to in enumerate((0, 1, pair, pair | 1))}
-
+    rows_of = [[] for _ in range(4)]
+    for total in total_of[:-1]:
+        crossed = swap(total[1::2], "tok", 1)
+        over = swap(jnp.stack([total[2], crossed[1]]), "tok", pair)
+        for r, got_rows in enumerate((total[0], crossed[0], over[0], over[1])):
+            rows_of[r].append(got_rows)
     shares, firsts = [], folded[:1]
     for x_side in (1, 0):
         even, odd = rest[2 * x_side:2 * x_side + 2]
@@ -345,9 +348,13 @@
             total = total[:, 0] + swap(total[:, 1], "hid", bit)
         shares.append(total[0])
     share = shares[1] + swap(shares[0], "tok", 1)
-    input_grad = share[0] + swap(share[1], "tok", pair)
-
-    quarters = [jnp.concatenate(rows_of, axis=1) for rows_of in handed.values()]
+    from_pair = swap(share[1], "tok", pair)
+    input_grad = share[0] + from_pair
+
+    for r, to in enumerate((0, 1, pair, pair | 1)):
+        rows_of[r].append(swap(after(total_of[-1][r], *([from_pair] if to & pair else [])), "tok", to) if to else total_of[-1][0])
+
+    quarters = [jnp.concatenate(pieces_of, axis=1) for pieces_of in rows_of]
     for bit in (1, 2):
         flip = mine & bit > 0
         quarters = [jnp.where(flip, quarters[j ^ bit], quarters[j]) for j in range(4)]

time: 240 us -> 248 us (1.033)
  waiting for transfers between devices: 133 us -> 157 us
  local copies, waits for them, and re-layouts: 23.3 us -> 10.4 us
  starting transfers between devices: 43.2 us -> 40.5 us
    ppermute x37 -> x35, waiting for transfers between devices: 133 us -> 157 us  [swap(): return lax.ppermute(value, axis, [(i, i ^ bit) for i in range(size)])]
    unnamed x84 -> x56, local copies, waits for them, and re-layouts: 20.4 us -> 6.34 us
    ppermute x37 -> x35, starting transfers between devices: 43.2 us -> 40.5 us  [swap(): return lax.ppermute(value, axis, [(i, i ^ bit) for i in range(size)])]
  transfers between devices with their start and end apart: 37 -> 35, of which waited for: 17 -> 23; matrix products, arithmetic and copies ran while one was open for 4% -> 4% of each run, Pallas kernels for 8% -> 8%
where the time goes in v1:
time: 248 us
  waiting for transfers between devices  157 us (63%)
  starting transfers between devices  40.5 us (16%)
  Pallas kernels  29.6 us (12%)
  local copies, waits for them, and re-layouts  10.4 us (4%)
  other arithmetic  9.18 us (4%)
    ppermute x35, waiting for transfers between devices, swap(): return lax.ppermute(value, axis, [(i, i ^ bit) for i in range(size)])  157 us
    ppermute x35, starting transfers between devices, swap(): return lax.ppermute(value, axis, [(i, i ^ bit) for i in range(size)])  40.5 us
    pallas_call x2, Pallas kernels, block_pass(): pl.pallas_call(functools.partial(kernel, cfg), out_shape=out, grid_spec=p...  29.6 us
    unnamed x56, local copies, waits for them, and re-layouts  6.34 us
  transfers between devices with their start and end apart: 35, of which 23 were waited for; matrix products, arithmetic and copies ran while one was open for 4% of the time, Pallas kernels for 8%

profile of v1, /device:TPU:0, one launch (start us, length us, event | category | flops | bytes accessed | tf_op | source)
XLA Modules:
  0.0 247.5 jit_solution(2820593541364380176)
XLA Ops:
  2.2 3.0 %collective-permute-start = (f32[2,128,1024]{2,1,0:T(8,128)S(1)}, f32[2,128,1024]{2,1,0:T(8,128)}, u32[]{:S(2)}, u32[]{:S(2)}) collective-permute-start(f32[2,128,1024]{2,1,0:T(8,128)S(1)} %pad_maximum_fusion.1), channel_id=1, source_target_pairs={{0,4},{4,0},{8,12},{12,8},{16,20},{20,16},{24,28},{28,24},{1,5},{5... | collective-permute-start | bytes 3145736 | tf_op jit(solution)/shard_map/ppermute | solution.py:17
  5.4 3.7 %collective-permute-start.1 = (f32[2,7,4,16,128]{4,3,2,1,0:T(8,128)S(1)}, f32[2,7,4,16,128]{4,3,2,1,0:T(8,128)S(1)}, u32[]{:S(2)}, u32[]{:S(2)}) collective-permute-start(f32[2,7,4,16,128]{4,3,2,1,0:T(8,128)S(1)} %pad_maximum_fusion.3), channel_id=1, source_target_pairs={{0,24},{4,28},{8,16},{12,20},{16,8},{20,12},{24,0},{28,4},{1,25},{... | collective-permute-start | bytes 1376264 | tf_op jit(solution)/shard_map/ppermute | solution.py:17
  9.1 11.6 %collective-permute-done.1.refs_20_ = f32[2,7,4,16,128]{4,3,2,1,0:T(8,128)S(1)} collective-permute-done((f32[2,7,4,16,128]{4,3,2,1,0:T(8,128)S(1)}, f32[2,7,4,16,128]{4,3,2,1,0:T(8,128)S(1)}, u32[]{:S(2)}, u32[]{:S(2)}) %collective-permute-start.1) | collective-permute-done | bytes 458784 | tf_op jit(solution)/shard_map/ppermute | solution.py:17
  20.7 7.7 %collective-permute-done.refs_2_ = f32[2,128,1024]{2,1,0:T(8,128)} collective-permute-done((f32[2,128,1024]{2,1,0:T(8,128)S(1)}, f32[2,128,1024]{2,1,0:T(8,128)}, u32[]{:S(2)}, u32[]{:S(2)}) %collective-permute-start) | collective-permute-done | bytes 1048608 | tf_op jit(solution)/shard_map/ppermute | solution.py:17
  28.4 1.8 collective-permute-start.3
  31.9 2.7 %collective-permute-start.6 = (f32[2,7,4,16,128]{4,3,2,1,0:T(8,128)S(1)}, f32[2,7,4,16,128]{4,3,2,1,0:T(8,128)S(1)}, u32[]{:S(2)}, u32[]{:S(2)}) collective-permute-start(f32[2,7,4,16,128]{4,3,2,1,0:T(8,128)S(1)} %pad_maximum_fusion.4.refs_14_), channel_id=1, source_target_pairs={{0,16},{4,20},{8,24},{12,28},{16,0},{20,4},{24,8},{28,12},{1,17},{... | collective-permute-start | bytes 1376264 | tf_op jit(solution)/shard_map/ppermute | solution.py:17
  34.6 15.4 %collective-permute-done.5.refs_6_ = f32[2,128,1024]{2,1,0:T(8,128)} collective-permute-done((f32[2,128,1024]{2,1,0:T(8,128)S(1)}, f32[2,128,1024]{2,1,0:T(8,128)}, u32[]{:S(2)}, u32[]{:S(2)}) %collective-permute-start.5) | collective-permute-done | bytes 1048608 | tf_op jit(solution)/shard_map/ppermute | solution.py:17
  56.2 2.5 %collective-permute-start.12 = (f32[2,7,4,16,128]{4,3,2,1,0:T(8,128)S(1)}, f32[2,7,4,16,128]{4,3,2,1,0:T(8,128)S(1)}, u32[]{:S(2)}, u32[]{:S(2)}) collective-permute-start(f32[2,7,4,16,128]{4,3,2,1,0:T(8,128)S(1)} %get-tuple-element.38), channel_id=1, source_target_pairs={{0,24},{4,28},{8,16},{12,20},{16,8},{20,12},{24,0},{28,4},{1,25},{... | collective-permute-start | bytes 1376264 | tf_op jit(solution)/shard_map/ppermute | solution.py:17
  58.8 8.3 %collective-permute-done.13.refs_16_ = f32[2,7,4,16,128]{4,3,2,1,0:T(8,128)S(1)} collective-permute-done((f32[2,7,4,16,128]{4,3,2,1,0:T(8,128)S(1)}, f32[2,7,4,16,128]{4,3,2,1,0:T(8,128)S(1)}, u32[]{:S(2)}, u32[]{:S(2)}) %collective-permute-start.13) | collective-permute-done | bytes 458784 | tf_op jit(solution)/shard_map/ppermute | solution.py:17
  67.1 9.6 %collective-permute-done.12.refs_21_ = f32[2,7,4,16,128]{4,3,2,1,0:T(8,128)S(1)} collective-permute-done((f32[2,7,4,16,128]{4,3,2,1,0:T(8,128)S(1)}, f32[2,7,4,16,128]{4,3,2,1,0:T(8,128)S(1)}, u32[]{:S(2)}, u32[]{:S(2)}) %collective-permute-start.12) | collective-permute-done | bytes 458784 | tf_op jit(solution)/shard_map/ppermute | solution.py:17
  79.6 2.6 %collective-permute-start.18 = (f32[2,7,4,16,128]{4,3,2,1,0:T(8,128)S(1)}, f32[2,7,4,16,128]{4,3,2,1,0:T(8,128)S(1)}, u32[]{:S(2)}, u32[]{:S(2)}) collective-permute-start(f32[2,7,4,16,128]{4,3,2,1,0:T(8,128)S(1)} %get-tuple-element.39.refs_15_), channel_id=1, source_target_pairs={{0,16},{4,20},{8,24},{12,28},{16,0},{20,4},{24,8},{28,12},{1,17},{... | collective-permute-start | bytes 1376264 | tf_op jit(solution)/shard_map/ppermute | solution.py:17
  82.7 15.6 %collective-permute-done.17.refs_17_ = f32[2,7,4,16,128]{4,3,2,1,0:T(8,128)S(1)} collective-permute-done((f32[2,7,4,16,128]{4,3,2,1,0:T(8,128)S(1)}, f32[2,7,4,16,128]{4,3,2,1,0:T(8,128)S(1)}, u32[]{:S(2)}, u32[]{:S(2)}) %collective-permute-start.17) | collective-permute-done | bytes 458784 | tf_op jit(solution)/shard_map/ppermute | solution.py:17
  98.3 1.7 collective-permute-done.18.refs_19_
  104.1 10.9 %shard_map.103 = (f32[4,2,2,4,16,128]{5,4,3,2,1,0:T(8,128)S(1)}, f32[4,2,2,4,16,128]{5,4,3,2,1,0:T(8,128)S(1)}, f32[32,512,128]{2,1,0:T(8,128)}) custom-call(s32[8]{0:T(128)S(1)} %reshape.30.up_at, s32[8]{0:T(128)S(1)} %reshape.31.down_at, s32[2]{0:T(128)S(1)} %pad_add_fusion.place, f32[128,4096]{1,0:T(8,128)} %refs_0_.3, f32[128,4096]{1,0:T(8,128)} %refs_1_.3, ...), custom_call_target="tpu_custom_call" | custom-call | flops 8053063680 | bytes 16777216 | tf_op jit(solution)/shard_map/pallas_call | solution.py:197
  119.9 18.7 %shard_map.104 = (f32[4,2,3,4,16,128]{5,4,3,2,1,0:T(8,128)S(1)}, f32[4,2,3,4,16,128]{5,4,3,2,1,0:T(8,128)S(1)}, f32[4,2,2,4,16,128]{5,4,3,2,1,0:T(8,128)S(1)}, f...) custom-call(s32[20]{0:T(128)S(1)} %reshape.28.up_at, ...), custom_call_target="tpu_custom_call" | custom-call | flops 20132659200 | bytes 16777216 | tf_op jit(solution)/shard_map/pallas_call | solution.py:197
  138.6 2.5 %collective-permute-done.19 = f32[4,2,2,4,16,128]{5,4,3,2,1,0:T(8,128)S(1)} collective-permute-done((f32[4,2,2,4,16,128]{5,4,3,2,1,0:T(8,128)S(1)}, f32[4,2,2,4,16,128]{5,4,3,2,1,0:T(8,128)S(1)}, u32[]{:S(2)}, u32[]{:S(2)}) %collective-permute-start.19) | collective-permute-done | bytes 524320 | tf_op jit(solution)/shard_map/ppermute | solution.py:17
  141.7 6.3 %collective-permute-done.22 = f32[2,2,128,1024]{3,2,1,0:T(8,128)S(1)} collective-permute-done((f32[2,2,128,1024]{3,2,1,0:T(8,128)S(1)}, f32[2,2,128,1024]{3,2,1,0:T(8,128)S(1)}, u32[]{:S(2)}, u32[]{:S(2)}) %collective-permute-start.22) | collective-permute-done | bytes 2097184 | tf_op jit(solution)/shard_map/ppermute | solution.py:17
  152.1 1.8 collective-permute-start.26
  153.9 2.0 add_bitcast_fusion.1
  157.2 19.2 %collective-permute-done.23 = f32[1,2,128,1024]{3,2,1,0:T(8,128)} collective-permute-done((f32[1,2,128,1024]{3,2,1,0:T(8,128)}, f32[1,2,128,1024]{3,2,1,0:T(8,128)}, u32[]{:S(2)}, u32[]{:S(2)}) %collective-permute-start.23) | collective-permute-done | bytes 1048608 | tf_op jit(solution)/shard_map/ppermute | solution.py:17
  177.7 1.6 collective-permute-start.24
  179.4 8.6 %collective-permute-done.28 = f32[4,2,3,4,16,128]{5,4,3,2,1,0:T(8,128)S(1)} collective-permute-done((f32[4,2,3,4,16,128]{5,4,3,2,1,0:T(8,128)}, f32[4,2,3,4,16,128]{5,4,3,2,1,0:T(8,128)S(1)}, u32[]{:S(2)}, u32[]{:S(2)}) %collective-permute-start.28) | collective-permute-done | bytes 786464 | tf_op jit(solution)/shard_map/ppermute | solution.py:17
  189.8 2.1 collective-permute-start.31
  191.9 17.8 %collective-permute-done.29 = f32[2,2,3,4,16,128]{5,4,3,2,1,0:T(8,128)S(1)} collective-permute-done((f32[2,2,3,4,16,128]{5,4,3,2,1,0:T(8,128)S(1)}, f32[2,2,3,4,16,128]{5,4,3,2,1,0:T(8,128)S(1)}, u32[]{:S(2)}, u32[]{:S(2)}) %collective-permute-start.29) | collective-permute-done | bytes 393248 | tf_op jit(solution)/shard_map/ppermute | solution.py:17
  210.3 2.1 collective-permute-start.25
  212.4 3.4 %collective-permute-done.31 = f32[4,2,2,4,16,128]{5,4,3,2,1,0:T(8,128)S(1)} collective-permute-done((f32[4,2,2,4,16,128]{5,4,3,2,1,0:T(8,128)S(1)}, f32[4,2,2,4,16,128]{5,4,3,2,1,0:T(8,128)S(1)}, u32[]{:S(2)}, u32[]{:S(2)}) %collective-permute-start.31) | collective-permute-done | bytes 524320 | tf_op jit(solution)/shard_map/ppermute | solution.py:17
  216.8 7.3 %collective-permute-done.30 = f32[2,2,3,4,16,128]{5,4,3,2,1,0:T(8,128)S(1)} collective-permute-done((f32[2,2,3,4,16,128]{5,4,3,2,1,0:T(8,128)S(1)}, f32[2,2,3,4,16,128]{5,4,3,2,1,0:T(8,128)S(1)}, u32[]{:S(2)}, u32[]{:S(2)}) %collective-permute-start.30) | collective-permute-done | bytes 393248 | tf_op jit(solution)/shard_map/ppermute | solution.py:17
  224.2 11.1 %collective-permute-done.25 = f32[128,1024]{1,0:T(8,128)S(1)} collective-permute-done((f32[128,1024]{1,0:T(8,128)S(1)}, f32[128,1024]{1,0:T(8,128)S(1)}, u32[]{:S(2)}, u32[]{:S(2)}) %collective-permute-start.25) | collective-permute-done | bytes 524320 | tf_op jit(solution)/shard_map/ppermute | solution.py:17
  235.3 2.4 collective-permute-start.32
  238.5 3.1 %collective-permute-done.33 = f32[2,2,4,16,128]{4,3,2,1,0:T(8,128)S(1)} collective-permute-done((f32[2,2,4,16,128]{4,3,2,1,0:T(8,128)S(1)}, f32[2,2,4,16,128]{4,3,2,1,0:T(8,128)S(1)}, u32[]{:S(2)}, u32[]{:S(2)}) %collective-permute-start.33) | collective-permute-done | bytes 131104 | tf_op jit(solution)/shard_map/ppermute | solution.py:17
  241.6 2.2 collective-permute-done.32
  245.9 1.6 fusion.6
  (144 shorter events, 35.6 us)
Async XLA Ops:
  2.2 26.3 %collective-permute-start = (f32[2,128,1024]{2,1,0:T(8,128)S(1)}, f32[2,128,1024]{2,1,0:T(8,128)}, u32[]{:S(2)}, u32[]{:S(2)}) collective-permute-start(f32[2,128,1024]{2,1,0:T(8,128)S(1)} %pad_maximum_fusion.1), channel_id=1, source_target_pairs={{0,4},{4,0},{8,12},{12,8},{16,20},{20,16},{24,28},{28,24},{1,5},{5... | collective-permute-start | bytes 3145736 | tf_op jit(solution)/shard_map/ppermute | solution.py:17
  5.4 15.3 %collective-permute-start.1 = (f32[2,7,4,16,128]{4,3,2,1,0:T(8,128)S(1)}, f32[2,7,4,16,128]{4,3,2,1,0:T(8,128)S(1)}, u32[]{:S(2)}, u32[]{:S(2)}) collective-permute-start(f32[2,7,4,16,128]{4,3,2,1,0:T(8,128)S(1)} %pad_maximum_fusion.3), channel_id=1, source_target_pairs={{0,24},{4,28},{8,16},{12,20},{16,8},{20,12},{24,0},{28,4},{1,25},{... | collective-permute-start | bytes 1376264 | tf_op jit(solution)/shard_map/ppermute | solution.py:17
  9.0 40.9 %collective-permute-start.5 = (f32[2,128,1024]{2,1,0:T(8,128)S(1)}, f32[2,128,1024]{2,1,0:T(8,128)}, u32[]{:S(2)}, u32[]{:S(2)}) collective-permute-start(f32[2,128,1024]{2,1,0:T(8,128)S(1)} %pad_maximum_fusion.1), channel_id=1, source_target_pairs={{0,8},{4,12},{8,0},{12,4},{16,24},{20,28},{24,16},{28,20},{1,9},{5... | collective-permute-start | bytes 3145736 | tf_op jit(solution)/shard_map/ppermute | solution.py:17
  28.4 25.1 %collective-permute-start.3 = (f32[2,128,1024]{2,1,0:T(8,128)}, f32[2,128,1024]{2,1,0:T(8,128)}, u32[]{:S(2)}, u32[]{:S(2)}) collective-permute-start(f32[2,128,1024]{2,1,0:T(8,128)} %collective-permute-done.refs_2_), channel_id=1, source_target_pairs={{0,2},{1,3},{2,0},{3,1},{4,6},{5,7},{6,4},{7,5},{8,10},{9,11},{10,... | collective-permute-start | bytes 3145736 | tf_op jit(solution)/shard_map/ppermute | solution.py:17
  30.3 21.0 %collective-permute-start.10 = (f32[2,2,7,4,16,128]{5,4,3,2,1,0:T(8,128)S(1)}, f32[2,2,7,4,16,128]{5,4,3,2,1,0:T(8,128)S(1)}, u32[]{:S(2)}, u32[]{:S(2)}) collective-permute-start(f32[2,2,7,4,16,128]{5,4,3,2,1,0:T(8,128)S(1)} %pad_maximum_fusion.2), channel_id=1, source_target_pairs={{0,4},{4,0},{8,12},{12,8},{16,20},{20,16},{24,28},{28,24},{1,5},{5... | collective-permute-start | bytes 2752520 | tf_op jit(solution)/shard_map/ppermute | solution.py:17
  31.9 21.7 %collective-permute-start.6 = (f32[2,7,4,16,128]{4,3,2,1,0:T(8,128)S(1)}, f32[2,7,4,16,128]{4,3,2,1,0:T(8,128)S(1)}, u32[]{:S(2)}, u32[]{:S(2)}) collective-permute-start(f32[2,7,4,16,128]{4,3,2,1,0:T(8,128)S(1)} %pad_maximum_fusion.4.refs_14_), channel_id=1, source_target_pairs={{0,16},{4,20},{8,24},{12,28},{16,0},{20,4},{24,8},{28,12},{1,17},{... | collective-permute-start | bytes 1376264 | tf_op jit(solution)/shard_map/ppermute | solution.py:17
  51.3 25.4 %collective-permute-start.11 = (f32[2,128,1024]{2,1,0:T(8,128)}, f32[2,128,1024]{2,1,0:T(8,128)}, u32[]{:S(2)}, u32[]{:S(2)}) collective-permute-start(f32[2,128,1024]{2,1,0:T(8,128)} %collective-permute-done.5.refs_6_), channel_id=1, source_target_pairs={{0,4},{4,0},{8,12},{12,8},{16,20},{20,16},{24,28},{28,24},{1,5},{5... | collective-permute-start | bytes 3145736 | tf_op jit(solution)/shard_map/ppermute | solution.py:17
  53.6 23.3 %collective-permute-start.8 = (f32[2,128,1024]{2,1,0:T(8,128)}, f32[2,128,1024]{2,1,0:T(8,128)}, u32[]{:S(2)}, u32[]{:S(2)}) collective-permute-start(f32[2,128,1024]{2,1,0:T(8,128)} %collective-permute-done.5.refs_6_), channel_id=1, source_target_pairs={{0,2},{1,3},{2,0},{3,1},{4,6},{5,7},{6,4},{7,5},{8,10},{9,11},{10,... | collective-permute-start | bytes 3145736 | tf_op jit(solution)/shard_map/ppermute | solution.py:17
  54.6 12.6 %collective-permute-start.13 = (f32[2,7,4,16,128]{4,3,2,1,0:T(8,128)S(1)}, f32[2,7,4,16,128]{4,3,2,1,0:T(8,128)S(1)}, u32[]{:S(2)}, u32[]{:S(2)}) collective-permute-start(f32[2,7,4,16,128]{4,3,2,1,0:T(8,128)S(1)} %pad_maximum_fusion.3), channel_id=1, source_target_pairs={{0,8},{4,12},{8,0},{12,4},{16,24},{20,28},{24,16},{28,20},{1,9},{5... | collective-permute-start | bytes 1376264 | tf_op jit(solution)/shard_map/ppermute | solution.py:17
  56.2 20.5 %collective-permute-start.12 = (f32[2,7,4,16,128]{4,3,2,1,0:T(8,128)S(1)}, f32[2,7,4,16,128]{4,3,2,1,0:T(8,128)S(1)}, u32[]{:S(2)}, u32[]{:S(2)}) collective-permute-start(f32[2,7,4,16,128]{4,3,2,1,0:T(8,128)S(1)} %get-tuple-element.38), channel_id=1, source_target_pairs={{0,24},{4,28},{8,16},{12,20},{16,8},{20,12},{24,0},{28,4},{1,25},{... | collective-permute-start | bytes 1376264 | tf_op jit(solution)/shard_map/ppermute | solution.py:17
  58.8 23.4 %collective-permute-start.2 = (f32[2,128,1024]{2,1,0:T(8,128)}, f32[2,128,1024]{2,1,0:T(8,128)S(1)}, u32[]{:S(2)}, u32[]{:S(2)}) collective-permute-start(f32[2,128,1024]{2,1,0:T(8,128)} %collective-permute-done.refs_2_), channel_id=1, source_target_pairs={{0,1},{1,0},{2,3},{3,2},{4,5},{5,4},{6,7},{7,6},{8,9},{9,8},{10,11... | collective-permute-start | bytes 3145736 | tf_op jit(solution)/shard_map/ppermute | solution.py:17
  76.8 23.7 %collective-permute-start.15 = (f32[2,128,1024]{2,1,0:T(8,128)}, f32[2,128,1024]{2,1,0:T(8,128)S(1)}, u32[]{:S(2)}, u32[]{:S(2)}) collective-permute-start(f32[2,128,1024]{2,1,0:T(8,128)} %collective-permute-done.11.refs_10_), channel_id=1, source_target_pairs={{0,2},{1,3},{2,0},{3,1},{4,6},{5,7},{6,4},{7,5},{8,10},{9,11},{10,... | collective-permute-start | bytes 3145736 | tf_op jit(solution)/shard_map/ppermute | solution.py:17
  78.1 20.1 %collective-permute-start.17 = (f32[2,7,4,16,128]{4,3,2,1,0:T(8,128)S(1)}, f32[2,7,4,16,128]{4,3,2,1,0:T(8,128)S(1)}, u32[]{:S(2)}, u32[]{:S(2)}) collective-permute-start(f32[2,7,4,16,128]{4,3,2,1,0:T(8,128)S(1)} %get-tuple-element.38), channel_id=1, source_target_pairs={{0,8},{4,12},{8,0},{12,4},{16,24},{20,28},{24,16},{28,20},{1,9},{5... | collective-permute-start | bytes 1376264 | tf_op jit(solution)/shard_map/ppermute | solution.py:17
  79.6 20.4 %collective-permute-start.18 = (f32[2,7,4,16,128]{4,3,2,1,0:T(8,128)S(1)}, f32[2,7,4,16,128]{4,3,2,1,0:T(8,128)S(1)}, u32[]{:S(2)}, u32[]{:S(2)}) collective-permute-start(f32[2,7,4,16,128]{4,3,2,1,0:T(8,128)S(1)} %get-tuple-element.39.refs_15_), channel_id=1, source_target_pairs={{0,16},{4,20},{8,24},{12,28},{16,0},{20,4},{24,8},{28,12},{1,17},{... | collective-permute-start | bytes 1376264 | tf_op jit(solution)/shard_map/ppermute | solution.py:17
  82.1 19.6 %collective-permute-start.7 = (f32[2,128,1024]{2,1,0:T(8,128)}, f32[2,128,1024]{2,1,0:T(8,128)}, u32[]{:S(2)}, u32[]{:S(2)}) collective-permute-start(f32[2,128,1024]{2,1,0:T(8,128)} %collective-permute-done.5.refs_6_), channel_id=1, source_target_pairs={{0,1},{1,0},{2,3},{3,2},{4,5},{5,4},{6,7},{7,6},{8,9},{9,8},{10,11... | collective-permute-start | bytes 3145736 | tf_op jit(solution)/shard_map/ppermute | solution.py:17
  82.2 19.6 %collective-permute-start.4 = (f32[2,128,1024]{2,1,0:T(8,128)}, f32[2,128,1024]{2,1,0:T(8,128)}, u32[]{:S(2)}, u32[]{:S(2)}) collective-permute-start(f32[2,128,1024]{2,1,0:T(8,128)} %collective-permute-done.3.refs_4_), channel_id=1, source_target_pairs={{0,1},{1,0},{2,3},{3,2},{4,5},{5,4},{6,7},{7,6},{8,9},{9,8},{10,11... | collective-permute-start | bytes 3145736 | tf_op jit(solution)/shard_map/ppermute | solution.py:17
  115.9 25.3 %collective-permute-start.19 = (f32[4,2,2,4,16,128]{5,4,3,2,1,0:T(8,128)S(1)}, f32[4,2,2,4,16,128]{5,4,3,2,1,0:T(8,128)S(1)}, u32[]{:S(2)}, u32[]{:S(2)}) collective-permute-start(f32[4,2,2,4,16,128]{5,4,3,2,1,0:T(8,128)S(1)} %get-tuple-element.43), channel_id=1, source_target_pairs={{0,16},{4,20},{8,24},{12,28},{16,0},{20,4},{24,8},{28,12},{1,17},{... | collective-permute-start | bytes 1572872 | tf_op jit(solution)/shard_map/ppermute | solution.py:17
  141.2 6.8 %collective-permute-start.22 = (f32[2,2,128,1024]{3,2,1,0:T(8,128)S(1)}, f32[2,2,128,1024]{3,2,1,0:T(8,128)S(1)}, u32[]{:S(2)}, u32[]{:S(2)}) collective-permute-start(f32[2,2,128,1024]{3,2,1,0:T(8,128)S(1)} %get-tuple-element.47), channel_id=1, source_target_pairs={{0,1},{1,0},{2,3},{3,2},{4,5},{5,4},{6,7},{7,6},{8,9},{9,8},{10,11... | collective-permute-start | bytes 6291464 | tf_op jit(solution)/shard_map/ppermute | solution.py:17
  141.2 12.7 %collective-permute-start.20 = (f32[2,2,128,1024]{3,2,1,0:T(8,128)}, f32[2,2,128,1024]{3,2,1,0:T(8,128)}, u32[]{:S(2)}, u32[]{:S(2)}) collective-permute-start(f32[2,2,128,1024]{3,2,1,0:T(8,128)} %get-tuple-element.44), channel_id=1, source_target_pairs={{0,1},{1,0},{2,3},{3,2},{4,5},{5,4},{6,7},{7,6},{8,9},{9,8},{10,11... | collective-permute-start | bytes 6291464 | tf_op jit(solution)/shard_map/ppermute | solution.py:17
  150.0 26.3 %collective-permute-start.23 = (f32[1,2,128,1024]{3,2,1,0:T(8,128)}, f32[1,2,128,1024]{3,2,1,0:T(8,128)}, u32[]{:S(2)}, u32[]{:S(2)}) collective-permute-start(f32[1,2,128,1024]{3,2,1,0:T(8,128)} %slice_bitcast_fusion), channel_id=1, source_target_pairs={{0,2},{1,3},{2,0},{3,1},{4,6},{5,7},{6,4},{7,5},{8,10},{9,11},{10,... | collective-permute-start | bytes 3145736 | tf_op jit(solution)/shard_map/ppermute | solution.py:17
  150.8 37.1 %collective-permute-start.28 = (f32[4,2,3,4,16,128]{5,4,3,2,1,0:T(8,128)}, f32[4,2,3,4,16,128]{5,4,3,2,1,0:T(8,128)S(1)}, u32[]{:S(2)}, u32[]{:S(2)}) collective-permute-start(f32[4,2,3,4,16,128]{5,4,3,2,1,0:T(8,128)} %copy-done.7), channel_id=1, source_target_pairs={{0,16},{4,20},{8,24},{12,28},{16,0},{20,4},{24,8},{28,12},{1,17},{... | collective-permute-start | bytes 2359304 | tf_op jit(solution)/shard_map/ppermute | solution.py:17
  152.1 37.5 %collective-permute-start.26 = (f32[2,2,2,4,16,128]{5,4,3,2,1,0:T(8,128)S(1)}, f32[2,2,2,4,16,128]{5,4,3,2,1,0:T(8,128)S(1)}, u32[]{:S(2)}, u32[]{:S(2)}) collective-permute-start(f32[2,2,2,4,16,128]{5,4,3,2,1,0:T(8,128)S(1)} %slice.94), channel_id=1, source_target_pairs={{0,4},{4,0},{8,12},{12,8},{16,20},{20,16},{24,28},{28,24},{1,5},{5... | collective-permute-start | bytes 786440 | tf_op jit(solution)/shard_map/ppermute | solution.py:17
  156.0 53.9 %collective-permute-start.21 = (f32[1,2,128,1024]{3,2,1,0:T(8,128)S(1)}, f32[1,2,128,1024]{3,2,1,0:T(8,128)S(1)}, u32[]{:S(2)}, u32[]{:S(2)}) collective-permute-start(f32[1,2,128,1024]{3,2,1,0:T(8,128)S(1)} %slice_bitcast_fusion.2), channel_id=1, source_target_pairs={{0,2},{1,3},{2,0},{3,1},{4,6},{5,7},{6,4},{7,5},{8,10},{9,11},{10,... | collective-permute-start | bytes 3145736 | tf_op jit(solution)/shard_map/ppermute | solution.py:17
  177.7 32.2 %collective-permute-start.24 = (f32[2,128,1024]{2,1,0:T(8,128)S(1)}, f32[2,128,1024]{2,1,0:T(8,128)S(1)}, u32[]{:S(2)}, u32[]{:S(2)}) collective-permute-start(f32[2,128,1024]{2,1,0:T(8,128)S(1)} %fusion.1), channel_id=1, source_target_pairs={{0,4},{4,0},{8,12},{12,8},{16,20},{20,16},{24,28},{28,24},{1,5},{5... | collective-permute-start | bytes 3145736 | tf_op jit(solution)/shard_map/ppermute | solution.py:17
  188.1 21.7 %collective-permute-start.29 = (f32[2,2,3,4,16,128]{5,4,3,2,1,0:T(8,128)S(1)}, f32[2,2,3,4,16,128]{5,4,3,2,1,0:T(8,128)S(1)}, u32[]{:S(2)}, u32[]{:S(2)}) collective-permute-start(f32[2,2,3,4,16,128]{5,4,3,2,1,0:T(8,128)S(1)} %slice.98), channel_id=1, source_target_pairs={{0,4},{4,0},{8,12},{12,8},{16,20},{20,16},{24,28},{28,24},{1,5},{5... | collective-permute-start | bytes 1179656 | tf_op jit(solution)/shard_map/ppermute | solution.py:17
  189.7 22.6 %collective-permute-start.27 = (f32[2,2,2,4,16,128]{5,4,3,2,1,0:T(8,128)S(1)}, f32[2,2,2,4,16,128]{5,4,3,2,1,0:T(8,128)S(1)}, u32[]{:S(2)}, u32[]{:S(2)}) collective-permute-start(f32[2,2,2,4,16,128]{5,4,3,2,1,0:T(8,128)S(1)} %pad_maximum_fusion.10), channel_id=1, source_target_pairs={{0,8},{4,12},{8,0},{12,4},{16,24},{20,28},{24,16},{28,20},{1,9},{5... | collective-permute-start | bytes 786440 | tf_op jit(solution)/shard_map/ppermute | solution.py:17
  189.8 25.9 %collective-permute-start.31 = (f32[4,2,2,4,16,128]{5,4,3,2,1,0:T(8,128)S(1)}, f32[4,2,2,4,16,128]{5,4,3,2,1,0:T(8,128)S(1)}, u32[]{:S(2)}, u32[]{:S(2)}) collective-permute-start(f32[4,2,2,4,16,128]{5,4,3,2,1,0:T(8,128)S(1)} %copy-done.9), channel_id=1, source_target_pairs={{0,16},{4,20},{8,24},{12,28},{16,0},{20,4},{24,8},{28,12},{1,17},{... | collective-permute-start | bytes 1572872 | tf_op jit(solution)/shard_map/ppermute | solution.py:17
  209.8 14.3 %collective-permute-start.30 = (f32[2,2,3,4,16,128]{5,4,3,2,1,0:T(8,128)S(1)}, f32[2,2,3,4,16,128]{5,4,3,2,1,0:T(8,128)S(1)}, u32[]{:S(2)}, u32[]{:S(2)}) collective-permute-start(f32[2,2,3,4,16,128]{5,4,3,2,1,0:T(8,128)S(1)} %pad_maximum_fusion.9), channel_id=1, source_target_pairs={{0,8},{4,12},{8,0},{12,4},{16,24},{20,28},{24,16},{28,20},{1,9},{5... | collective-permute-start | bytes 1179656 | tf_op jit(solution)/shard_map/ppermute | solution.py:17
  210.3 25.0 %collective-permute-start.25 = (f32[128,1024]{1,0:T(8,128)S(1)}, f32[128,1024]{1,0:T(8,128)S(1)}, u32[]{:S(2)}, u32[]{:S(2)}) collective-permute-start(f32[128,1024]{1,0:T(8,128)S(1)} %slice_bitcast_fusion.4), channel_id=1, source_target_pairs={{0,8},{4,12},{8,0},{12,4},{16,24},{20,28},{24,16},{28,20},{1,9},{5... | collective-permute-start | bytes 1572872 | tf_op jit(solution)/shard_map/ppermute | solution.py:17
  215.9 22.6 %collective-permute-start.34 = (f32[2,2,4,16,128]{4,3,2,1,0:T(8,128)S(1)}, f32[2,2,4,16,128]{4,3,2,1,0:T(8,128)S(1)}, u32[]{:S(2)}, u32[]{:S(2)}) collective-permute-start(f32[2,2,4,16,128]{4,3,2,1,0:T(8,128)S(1)} %get-tuple-element.74), channel_id=1, source_target_pairs={{0,4},{4,0},{8,12},{12,8},{16,20},{20,16},{24,28},{28,24},{1,5},{5... | collective-permute-start | bytes 393224 | tf_op jit(solution)/shard_map/ppermute | solution.py:17
  235.3 6.4 %collective-permute-start.33 = (f32[2,2,4,16,128]{4,3,2,1,0:T(8,128)S(1)}, f32[2,2,4,16,128]{4,3,2,1,0:T(8,128)S(1)}, u32[]{:S(2)}, u32[]{:S(2)}) collective-permute-start(f32[2,2,4,16,128]{4,3,2,1,0:T(8,128)S(1)} %get-tuple-element.56), channel_id=1, source_target_pairs={{0,8},{4,12},{8,0},{12,4},{16,24},{20,28},{24,16},{28,20},{1,9},{5... | collective-permute-start | bytes 393224 | tf_op jit(solution)/shard_map/ppermute | solution.py:17
  235.3 8.6 %collective-permute-start.32 = (f32[2,2,4,16,128]{4,3,2,1,0:T(8,128)S(1)}, f32[2,2,4,16,128]{4,3,2,1,0:T(8,128)S(1)}, u32[]{:S(2)}, u32[]{:S(2)}) collective-permute-start(f32[2,2,4,16,128]{4,3,2,1,0:T(8,128)S(1)} %get-tuple-element.55), channel_id=1, source_target_pairs={{0,12},{4,8},{8,4},{12,0},{16,28},{20,24},{24,20},{28,16},{1,13},{... | collective-permute-start | bytes 393224 | tf_op jit(solution)/shard_map/ppermute | solution.py:17
  (31 other events, 497.9 us)
